TPU v7x, 32 devices: a whole 2x2x4 slice. The times are simulated.
32 devices in a mesh: groups: 2 (over y), head: 16 (over z, x, core).
Axes of the slice: x: 2, y: 2, z: 4, core: 2. Of those that a mesh axis runs over, the one named last changes fastest.
Arguments:
- tokens: bfloat16 [768, 8192], P('groups', 'head'), parts along dimension 0, may hold values from -6 to 6
- segment_ids: int32 [768], P('groups'), parts along dimension 0, may hold values from 0 to 5, never falling along the last dimension, each value on 1 to 96 neighbouring positions
- in_weight: bfloat16 [8192, 8192], P('head'), may hold values from -0.0625 to 0.0625
- dt_weight: bfloat16 [8192, 16], P(None, 'head'), may hold values from -0.0625 to 0.0625
- conv_weight: float32 [4, 6144], P(None, 'head'), may hold values from -3 to 3
- conv_bias: float32 [6144], P('head'), may hold values from -0.5 to 0.5
- a_rate: float32 [16], P('head'), may hold values from 0.003 to 0.1
- dt_bias: float32 [16], P('head'), may hold values from -1.5 to 0.5
- out_weight: bfloat16 [2048, 8192], P(None, 'head'), may hold values from -0.1875 to 0.1875
Outputs:
- mixed_out: bfloat16 [768, 8192], P('groups', 'head'), parts along dimension 0
There are 2 independent parts, one for each index of `groups`. A program takes and returns all parts, laid end to end along the dimension named above; an argument that names none is the same for every part. Nothing has to cross between parts.
Inputs may be any that keep to these rules, and one draw needn't show every extreme that they name: `segment_ids`: never falls along the sequence; each value marks one document of 1 to 96 consecutive positions.
All inputs are finite; a program needn't handle non-finite values.
Results may differ from a plain program's by a relative error of at most 0.0046.
The roundings to bfloat16 on the way count: a program that leaves them out, or rounds other values in their place, can miss the bound.
Values may be sent and summed in bfloat16 or wider, within the bound.
A program may use at most 128 MiB of HBM per device.

v0:
```python
import jax
import jax.numpy as jnp
from jax import lax
from jax.sharding import PartitionSpec as P

HEAD_DIM = 128
STATE = 128
CONV = 4
BLOCK = 128


def causal_mix(conv_in, segment_ids, conv_weight, conv_bias):
    positions = conv_in.shape[0]
    running = conv_bias[None, :] + conv_weight[CONV - 1][None, :] * conv_in
    for offset in range(1, CONV):
        earlier = jnp.concatenate(
            [jnp.zeros((offset, conv_in.shape[1]), conv_in.dtype), conv_in[: positions - offset]],
            axis=0,
        )
        earlier_seg = jnp.concatenate(
            [jnp.full((offset,), -1, jnp.int32), segment_ids[: positions - offset]], axis=0
        )
        usable = (earlier_seg == segment_ids).astype(conv_in.dtype)
        running = running + conv_weight[CONV - 1 - offset][None, :] * earlier * usable[:, None]
    return jax.nn.silu(running)


def block_scan(x_part, b_part, c_part, step_size, a_rate, segment_ids):
    length, heads_here, _ = x_part.shape
    blocks_count = length // BLOCK
    top = lax.Precision.HIGHEST
    log_decay = (-a_rate[None, :] * step_size).reshape(blocks_count, BLOCK, heads_here)
    cumulative = jnp.cumsum(log_decay, axis=1)
    seg_blocks = segment_ids.reshape(blocks_count, BLOCK)
    x_scaled = (x_part * step_size[:, :, None]).reshape(blocks_count, BLOCK, heads_here, HEAD_DIM)
    b_blocks = b_part.reshape(blocks_count, BLOCK, heads_here, STATE)
    c_blocks = c_part.reshape(blocks_count, BLOCK, heads_here, STATE)
    within = jnp.arange(BLOCK)
    causal = within[:, None] >= within[None, :]
    allowed = (causal[None] & (seg_blocks[:, :, None] == seg_blocks[:, None, :]))[..., None]
    log_gap = cumulative[:, :, None, :] - cumulative[:, None, :, :]
    weights = jnp.where(allowed, jnp.exp(jnp.where(allowed, log_gap, 0.0)), 0.0)
    scores = jnp.einsum("kthn,kshn->ktsh", c_blocks, b_blocks, precision=top)
    y_inner = jnp.einsum("ktsh,kshp->kthp", scores * weights, x_scaled, precision=top)
    last_seg = seg_blocks[:, -1]
    end_weight = (
        jnp.exp(cumulative[:, -1:, :] - cumulative)
        * (seg_blocks == last_seg[:, None]).astype(jnp.float32)[:, :, None]
    )
    local_state = jnp.einsum(
        "kshp,kshn->khpn", x_scaled * end_weight[..., None], b_blocks, precision=top
    )
    prev_seg = jnp.concatenate([jnp.full((1,), -1, jnp.int32), last_seg[:-1]])
    through = (last_seg == prev_seg).astype(jnp.float32)[:, None] * jnp.exp(cumulative[:, -1, :])

    def pass_on(carried, inputs):
        through_block, local_block = inputs
        return (through_block[:, None, None] * carried + local_block, carried)

    zero_state = jnp.zeros((heads_here, HEAD_DIM, STATE), jnp.float32)
    _, entering = lax.scan(pass_on, zero_state, (through, local_state))
    reaches = (seg_blocks == prev_seg[:, None]).astype(jnp.float32)[:, :, None] * jnp.exp(
        cumulative
    )
    y_carry = reaches[..., None] * jnp.einsum("kthn,khpn->kthp", c_blocks, entering, precision=top)
    return (y_inner + y_carry).reshape(length, heads_here, HEAD_DIM)


def body(
    tokens, segment_ids, in_weight, dt_weight, conv_weight, conv_bias, a_rate, dt_bias, out_weight
):
    length = tokens.shape[0]
    heads_here = dt_weight.shape[1]
    proj_width = 2 * HEAD_DIM + 2 * STATE
    conv_chan = HEAD_DIM + 2 * STATE
    dt_rows = lax.all_to_all(dt_weight, "head", split_axis=0, concat_axis=1, tiled=True)
    proj_part = jnp.dot(tokens, in_weight, preferred_element_type=jnp.float32)
    step_part = jnp.dot(tokens, dt_rows, preferred_element_type=jnp.float32)
    proj_sum = lax.psum_scatter(proj_part, "head", scatter_dimension=1, tiled=True)
    step_sum = lax.psum_scatter(step_part, "head", scatter_dimension=1, tiled=True)
    projected = (
        lax.optimization_barrier(proj_sum.astype(jnp.bfloat16))
        .astype(jnp.float32)
        .reshape(length, heads_here, proj_width)
    )
    gate_part = projected[:, :, HEAD_DIM : 2 * HEAD_DIM]
    conv_in = jnp.concatenate(
        [projected[:, :, :HEAD_DIM], projected[:, :, 2 * HEAD_DIM :]], axis=2
    ).reshape(length, heads_here * conv_chan)
    conv_out = causal_mix(conv_in, segment_ids, conv_weight, conv_bias).reshape(
        length, heads_here, conv_chan
    )
    step_size = jax.nn.softplus(step_sum + dt_bias[None, :])
    ssd_out = block_scan(
        conv_out[:, :, :HEAD_DIM],
        conv_out[:, :, HEAD_DIM : HEAD_DIM + STATE],
        conv_out[:, :, HEAD_DIM + STATE :],
        step_size,
        a_rate,
        segment_ids,
    )
    gated = ssd_out * jax.nn.silu(gate_part)
    normed = (gated * lax.rsqrt(jnp.mean(gated * gated, axis=2, keepdims=True) + 1e-05)).astype(
        jnp.bfloat16
    )
    normed = normed.reshape(length, heads_here * HEAD_DIM)
    all_normed = lax.all_gather(normed, "head", axis=1, tiled=True)
    mixed_out = jnp.dot(all_normed, out_weight, preferred_element_type=jnp.float32)
    return mixed_out.astype(jnp.bfloat16)


def solution(mesh):
    return jax.shard_map(
        body,
        mesh=mesh,
        in_specs=(
            P("groups", "head"),
            P("groups"),
            P("head", None),
            P(None, "head"),
            P(None, "head"),
            P("head"),
            P("head"),
            P("head"),
            P(None, "head"),
        ),
        out_specs=P("groups", "head"),
        check_vma=False,
    )
```

profile of v0, /device:TPU:1, one launch (start us, length us, event | category | flops | bytes accessed | tf_op | source)
XLA Modules:
  0.0 223.8 jit_solution(15310387544877214040)
XLA Ops:
  6.5 0.0 copy-start
  6.5 0.0 reduce-scatter.2.cloned.1.call-start
  6.5 11.6 %fusion.31 = f32[384,8192]{1,0:T(8,128)} fusion(bf16[384,512]{1,0:T(8,128)(2,1)} %param.11, bf16[512,8192]{1,0:T(8,128)(2,1)} %param.13), kind=kOutput, calls=%fused_computation.70 | convolution fusion | flops 3221225472 | bytes 21364736 | tf_op jit(solution)/shard_map/dot_general | solution.py:77
  18.2 0.0 copy-start.3
  18.2 0.0 copy-start.2
  18.2 0.0 copy-start.4
  18.2 0.0 copy-start.6
  18.2 0.0 copy-start.1
  18.2 0.0 reduce-scatter.2.cloned.1.call-update
  18.2 0.5 broadcast.187
  18.8 0.2 copy-done.3
  18.9 0.7 reduce.20
  19.7 0.6 reshape.281
  20.3 7.3 %all-to-all-start = ((bf16[16,2,256]{2,1,0:T(2,128)(2,1)}), bf16[16,2,256]{2,1,0:T(2,128)(2,1)S(1)}, u32[]{:S(2)}, u32[]{:S(2)}) async-start(bf16[16,2,256]{2,1,0:T(2,128)(2,1)} %reshape.281), calls=%async_computation.1 | async-start | bytes 32768 | tf_op jit(solution)/shard_map/all_to_all | solution.py:76
  27.6 0.0 all-gather.3.cloned.1.call-start
  27.7 0.0 copy-done.2
  27.7 0.2 slice_reduce_fusion
  27.8 0.6 iota_compare_fusion
  28.5 0.0 copy-done.4
  28.5 0.2 slice_reduce_fusion.6
  28.7 0.1 fusion.29
  28.8 0.1 pad_add_fusion
  30.2 0.0 copy-done.6
  30.2 0.7 dynamic-slice
  30.8 2.6 %all-to-all-done = bf16[16,2,256]{2,1,0:T(2,128)(2,1)S(1)} async-done(((bf16[16,2,256]{2,1,0:T(2,128)(2,1)}), bf16[16,2,256]{2,1,0:T(2,128)(2,1)S(1)}, u32[]{:S(2)}, u32[]{:S(2)}) %all-to-all-start) | async-done | bytes 16416 | tf_op jit(solution)/shard_map/all_to_all | solution.py:76
  33.5 0.0 copy-done.1
  33.5 0.2 fusion.24
  33.7 56.5 %all-reduce.5 = f32[384,16]{0,1:T(8,128)S(1)} all-reduce(f32[384,16]{0,1:T(8,128)S(1)} %fusion.24), channel_id=4, replica_groups=mesh['groups'=2,'head'=16] {'head'}, use_global_device_ids=true, to_apply=%region_1.0.clone | all-reduce | flops 6144 | bytes 49152
  90.2 0.7 fusion.30
  91.0 0.2 reshape.269
  91.2 0.2 reduce_window_sum.11
  91.4 0.1 reduce.7
  91.5 0.1 slice_reduce_fusion.5
  91.6 0.7 bitcast_select_fusion
  92.3 0.7 exponential_select_fusion.1
  93.0 61.7 %reduce-scatter.2.cloned.1.call-done = f32[384,512]{1,0:T(8,128)} async-done(((f32[384,8192]{1,0:T(8,128)}), f32[384,512]{1,0:T(8,128)}) %reduce-scatter.2.cloned.1.call-update) | async-done | bytes 786448 | tf_op jit(solution)/shard_map/reduce_scatter | solution.py:79
  154.7 1.2 convert_element_type.27
  155.9 0.1 bitcast_convert_fusion
  156.0 0.0 copy-start.5
  156.2 0.5 copy-done.5
  156.7 0.5 multiply_bitcast_fusion
  157.1 0.1 slice_multiply_fusion
  157.3 0.8 copy.43
  158.1 1.9 convolution_bitcast_fusion.1
  160.0 10.1 %while.13 = (s32[]{:T(128)}, f32[1,128,128]{2,1,0:T(8,128)S(1)}, f32[3,1,128,128]{3,2,1,0:T(8,128)}, f32[3,1]{1,0:T(4,128)}, f32[3,1,128,128]{3,2,1,0:T(8,128)}, /*index=5*/s32[]{:T(128)}, s32[]{:T(128)}) while((s32[]{:T(128)}, f32[1,128,128]{2,1,0:T(8,128)S(1)}, f32[3,1,128,128]{3,2,1,0:T(8,128)}, f32[3,1]{1,0:T(4,128)}, ...), condition=%wide.region_4.5_spmd.clone, body=%wide.region_3.4_spmd.clone.sunk | while | flops 65539 | bytes 328300 | solution.py:61
  160.0 0.6 bitcast_dynamic-update-slice_fusion.2
  160.7 1.3 constant_dynamic-slice_fusion.2
  161.9 1.5 bitcast_add_fusion.2
  163.4 0.6 bitcast_dynamic-update-slice_fusion.2
  164.1 1.3 constant_dynamic-slice_fusion.2
  165.3 1.5 bitcast_add_fusion.2
  166.8 0.6 bitcast_dynamic-update-slice_fusion.2
  167.4 1.3 constant_dynamic-slice_fusion.2
  168.7 1.5 bitcast_add_fusion.2
  170.2 1.3 fusion.7
  171.4 1.5 fusion.8
  172.9 0.5 fusion.5
  173.4 0.2 multiply_reduce_fusion
  173.6 0.8 multiply_convert_fusion
  174.3 0.0 all-gather.3.cloned.1.call-update
  174.4 39.5 %all-gather.3.cloned.1.call-done = bf16[384,1,2048]{2,0,1:T(8,128)(2,1)} async-done(((bf16[384,1,128]{2,0,1:T(8,128)(2,1)}), bf16[384,1,2048]{2,0,1:T(8,128)(2,1)}) %all-gather.3.cloned.1.call-update) | async-done | bytes 1572880 | tf_op jit(solution)/shard_map/all_gather | solution.py:107
  213.8 0.0 copy-done
  213.8 3.1 %fusion.2 = bf16[384,512]{1,0:T(8,128)(2,1)} fusion(bf16[2048,512]{1,0:T(8,128)(2,1)S(1)} %copy-done, bf16[384,1,2048]{2,0,1:T(8,128)(2,1)} %all-gather.3.cloned.1.call-done), kind=kOutput, calls=%fused_computation.5 | convolution fusion | flops 805502976 | bytes 4063232 | tf_op jit(solution)/shard_map/dot_general | solution.py:108
  (10 shorter events, 0.2 us)
Async XLA Ops:
  6.5 207.3 %copy-start = (bf16[2048,512]{1,0:T(8,128)(2,1)S(1)}, bf16[2048,512]{1,0:T(8,128)(2,1)}, u32[]{:S(2)}) copy-start(bf16[2048,512]{1,0:T(8,128)(2,1)} %param.19) | copy-start | bytes 6291460
  6.5 148.2 %reduce-scatter.2.cloned.1.call-start = ((), (), s32[]{:S(2)}) async-start(), calls=%async_computation.2 | async-start | bytes 13369344 | tf_op jit(solution)/shard_map/reduce_scatter | solution.py:79
  18.2 0.8 copy-start.3
  18.2 9.5 %copy-start.2 = (s32[384]{0:T(512)S(1)}, s32[384]{0:T(512)}, u32[]{:S(2)}) copy-start(s32[384]{0:T(512)} %param.12) | copy-start | bytes 4612
  18.2 10.3 %copy-start.4 = (f32[4,384]{1,0:T(4,128)S(1)}, f32[4,384]{1,0:T(4,128)}, u32[]{:S(2)}) copy-start(f32[4,384]{1,0:T(4,128)} %param.15) | copy-start | bytes 18436
  18.2 12.0 %copy-start.6 = (u32[32]{0:T(128)S(1)}, u32[32]{0:T(128)}, u32[]{:S(2)}) copy-start(u32[32]{0:T(128)} %constant.60) | copy-start | bytes 388
  18.2 15.3 %copy-start.1 = (bf16[384,512]{1,0:T(8,128)(2,1)S(1)}, bf16[384,512]{1,0:T(8,128)(2,1)}, u32[]{:S(2)}) copy-start(bf16[384,512]{1,0:T(8,128)(2,1)} %param.11) | copy-start | bytes 1179652
  20.3 13.2 %all-to-all-start = ((bf16[16,2,256]{2,1,0:T(2,128)(2,1)}), bf16[16,2,256]{2,1,0:T(2,128)(2,1)S(1)}, u32[]{:S(2)}, u32[]{:S(2)}) async-start(bf16[16,2,256]{2,1,0:T(2,128)(2,1)} %reshape.281), calls=%async_computation.1 | async-start | bytes 32768 | tf_op jit(solution)/shard_map/all_to_all | solution.py:76
  27.6 186.2 %all-gather.3.cloned.1.call-start = ((), (), s32[]{:S(2)}) async-start(), calls=%async_computation.3 | async-start | bytes 1671168 | tf_op jit(solution)/shard_map/all_gather | solution.py:107
  156.0 0.7 copy-start.5
Sparse Core Ops, SparseCore 0:
  18.4 136.2 reduce-scatter.1
  174.5 39.2 all-gather.2
where the time goes:
time: 225 us; the launch traced here: 224 us
  waiting for transfers between devices  104 us (46%)
  blocking collectives  56.5 us (25%)
  matrix products  20.2 us (9%)
  between operations  14.9 us (7%)
  other arithmetic  13.1 us (6%)
  local copies, waits for them, and re-layouts  7.84 us (3%)
  starting transfers between devices  7.36 us (3%)
    reduce_scatter x1, waiting for transfers between devices, body(): lax.psum_scatter(proj_part, 'head', scatter_dimension=1, tiled=True)  61.7 us
    unnamed x1, blocking collectives  56.5 us
    all_gather x1, waiting for transfers between devices, body(): all_normed = lax.all_gather(normed, 'head', axis=1, tiled=True)  39.5 us
    dot_general x1, matrix products, body(): proj_part = jnp.dot(tokens, in_weight, preferred_element_type=jnp.float32)  11.6 us
    all_to_all x1, starting transfers between devices, body(): lax.all_to_all(dt_weight, 'head', split_axis=0, concat_axis=1, tiled=True)  7.32 us
  transfers between devices with their start and end apart: 3, of which 3 were waited for; matrix products, arithmetic and copies ran while one was open for 3% of the time, Pallas kernels for 0%

commit v1 on v0

--- a/solution.py
+++ b/solution.py
@@ -1,6 +1,8 @@
 import jax
 import jax.numpy as jnp
 from jax import lax
+from jax.experimental import pallas as pl
+from jax.experimental.pallas import tpu as pltpu
 from jax.sharding import PartitionSpec as P
 
 HEAD_DIM = 128
@@ -109,9 +111,398 @@
     return mixed_out.astype(jnp.bfloat16)
 
 
+CHUNK = 128
+BLOCK_COLS = 2 * HEAD_DIM + 2 * STATE
+CODE_STEP = 1170.0
+CODE_LOW = 16.0
+LN2 = 0.6931471805599453
+MESH = pl.DeviceIdType.MESH
+
+
+def encode(value):
+    level = jnp.log(jnp.maximum(jnp.abs(value), 2.0**-CODE_LOW)) * (CODE_STEP / LN2) + CODE_LOW * CODE_STEP
+    level = jnp.minimum(jnp.round(level), 32767.0)
+    return jnp.where(value < 0, -level, level).astype(jnp.int32).astype(jnp.int16)
+
+
+def decode(code):
+    level = code.astype(jnp.int32).astype(jnp.float32)
+    size = jnp.exp(jnp.abs(level) * (LN2 / CODE_STEP) - CODE_LOW * LN2)
+    return jnp.where(level < 0, -size, jnp.where(level > 0, size, 0.0))
+
+
+def fused(
+    tok_ref, w_ref, dtw_ref, segc_ref, segr_ref, cw_ref, cb_ref, par_ref, ow_ref, out_ref,
+    tok, wbuf, owbuf, dtw, pdt_out, pdt_in, xs, xr, zs, ur, dr, acc, part, conv, gate, gat, state,
+    loc_sem, wsend, wrecv, tsem, dws, dwr, pds, pdr, xss, xrs, zss, urs, drs, gsend, grecv,
+):
+    chunks = tok_ref.shape[0] // CHUNK
+    heads = dtw_ref.shape[0]
+    depth = tok_ref.shape[1]
+    me = lax.axis_index("head")
+    core = me % 2
+    x = (me // 2) % 2
+    z = me // 4
+    sib = me + 1 - 2 * core
+    xnb = me + 2 - 4 * x
+    up_dev = me + 4
+    down_dev = me - 4
+
+    def order(k):
+        return lax.rem(lax.div(jnp.int32((15, 114, 153, 228)[k]), lax.select(z == 0, 1, lax.select(z == 1, 4, lax.select(z == 2, 16, 64)))), 4)
+
+    def head_of(xx, zz, cc):
+        return zz * 4 + xx * 2 + cc
+
+    def remote(src, dst, ss, rs, dev):
+        return pltpu.make_async_remote_copy(
+            src_ref=src, dst_ref=dst, send_sem=ss, recv_sem=rs, device_id={"head": dev}, device_id_type=MESH
+        )
+
+    barrier = pltpu.get_barrier_semaphore()
+    for step in range(1, heads):
+        pl.semaphore_signal(barrier, inc=1, device_id={"head": lax.rem(me + step, heads)}, device_id_type=MESH)
+
+    def local_w(k, side):
+        col = head_of(1 - x if side == 0 else x, order(k), core) * BLOCK_COLS
+        slot = side * 4 + k
+        return pltpu.make_async_copy(
+            w_ref.at[:, pl.ds(pl.multiple_of(col, BLOCK_COLS), BLOCK_COLS)], wbuf.at[slot, pl.ds(0, depth)], loc_sem.at[slot]
+        )
+
+    def sib_w(k, side):
+        col = head_of(1 - x if side == 0 else x, order(k), 1 - core) * BLOCK_COLS
+        slot = side * 4 + k
+        return remote(
+            w_ref.at[:, pl.ds(pl.multiple_of(col, BLOCK_COLS), BLOCK_COLS)],
+            wbuf.at[slot, pl.ds(depth, depth)], wsend.at[slot], wrecv.at[slot], sib,
+        )
+
+    pairs = [(k, side) for side in range(2) for k in range(4)]
+    local_tok = pltpu.make_async_copy(tok_ref, tok.at[0], loc_sem.at[8])
+    local_tok.start()
+    for k, side in pairs:
+        local_w(k, side).start()
+    local_ow = pltpu.make_async_copy(ow_ref, owbuf, loc_sem.at[9])
+    local_ow.start()
+    pl.semaphore_wait(barrier, heads - 1)
+
+    sib_tok = remote(tok_ref, tok.at[1], tsem.at[0], tsem.at[1], sib)
+    sib_tok.start()
+    for k, side in pairs:
+        sib_w(k, side).start()
+
+    def dtw_copy(step, incoming):
+        other = lax.rem(me + step, heads)
+        return remote(dtw_ref.at[other], dtw.at[other if incoming else me], dws.at[step], dwr.at[heads - step if incoming else step], other)
+
+    for step in range(1, heads):
+        dtw_copy(step, False).start()
+    own_dtw = pltpu.make_async_copy(dtw_ref.at[me], dtw.at[me], loc_sem.at[10])
+    own_dtw.start()
+    local_tok.wait()
+    sib_tok.wait_recv()
+
+    def product(slot, r):
+        rows = pl.ds(r * CHUNK, CHUNK)
+        return jnp.dot(tok[0, rows, :], wbuf[slot, :depth], preferred_element_type=jnp.float32) + jnp.dot(
+            tok[1, rows, :], wbuf[slot, depth:], preferred_element_type=jnp.float32
+        )
+
+    def x_copy(r, k):
+        return remote(xs.at[r, k], xr.at[r, k], xss.at[r, k], xrs.at[r, k], xnb)
+
+    def z_copy(r, d, k, buf, sems, dev):
+        return remote(zs.at[r, k], buf.at[r, d], zss.at[r, k], sems.at[r, d], dev)
+
+    def x_phase(r):
+        for k in range(4):
+            if r == 0:
+                local_w(k, 0).wait()
+                sib_w(k, 0).wait_recv()
+            xs[r, k] = encode(product(k, r))
+            x_copy(r, k).start()
+
+    def z_phase(r):
+        for k in range(4):
+            if r == 0:
+                local_w(k, 1).wait()
+                sib_w(k, 1).wait_recv()
+            d = order(k)
+            mine = product(4 + k, r)
+            x_copy(r, k).wait_recv()
+            mine = mine + decode(xr[r, k])
+            if k == 3:
+                acc[r] = mine
+            else:
+                part[...] = mine
+                for buf, sems, dev, here, first in (
+                    (ur, urs, up_dev, d > z, z == 0),
+                    (dr, drs, down_dev, d < z, z == 3),
+                ):
+
+                    @pl.when(here)
+                    def _(buf=buf, sems=sems, dev=dev, first=first):
+                        @pl.when(jnp.logical_not(first))
+                        def _():
+                            z_copy(r, d, k, buf, sems, dev).wait_recv()
+                            part[...] += decode(buf[r, d])
+
+                        zs[r, k] = encode(part[...])
+                        z_copy(r, d, k, buf, sems, dev).start()
+
+    def pdt_copy(step, incoming):
+        other = lax.rem(me + step, heads)
+        return remote(pdt_out.at[other], pdt_in.at[other if incoming else me], pds.at[step], pdr.at[heads - step if incoming else step], other)
+
+    def step_phase():
+        own_dtw.wait()
+        for step in range(1, heads):
+            dtw_copy(step, True).wait_recv()
+        total = jnp.zeros((heads, tok_ref.shape[0]), jnp.float32)
+        for j in range(depth // 128):
+            total = total + lax.dot_general(
+                dtw[:, j, :].astype(jnp.bfloat16), tok[0, :, j * 128 : (j + 1) * 128],
+                (((1,), (1,)), ((), ())), preferred_element_type=jnp.float32,
+            )
+        for r in range(chunks):
+            pdt_out[:, r, :] = total[:, r * CHUNK : (r + 1) * CHUNK]
+        for r in range(chunks, 8):
+            pdt_out[:, r, :] = jnp.zeros((heads, 128), jnp.float32)
+        for step in range(1, heads):
+            pdt_copy(step, False).start()
+        own = pltpu.make_async_copy(pdt_out.at[me], pdt_in.at[me], loc_sem.at[11])
+        own.start()
+        own.wait()
+
+    top = lax.Precision.HIGHEST
+
+    def dot32(a, b, dims):
+        return lax.dot_general(a, b, (dims, ((), ())), precision=top, preferred_element_type=jnp.float32)
+
+    def block_phase(r):
+        for edge, buf, sems, dev in ((0, ur, urs, up_dev), (3, dr, drs, down_dev)):
+
+            @pl.when(z != edge)
+            def _(buf=buf, sems=sems, dev=dev):
+                z_copy(r, z, 3, buf, sems, dev).wait_recv()
+                acc[r] += decode(buf[r, z])
+
+        gate[...] = acc[r].astype(jnp.bfloat16)
+        projected = gate[...].astype(jnp.float32)
+        base = 8 + r * CHUNK
+        conv[base : base + CHUNK, :HEAD_DIM] = projected[:, :HEAD_DIM]
+        conv[base : base + CHUNK, HEAD_DIM:] = projected[:, 2 * HEAD_DIM :]
+        gate_part = projected[:, HEAD_DIM : 2 * HEAD_DIM]
+        seg_col = segc_ref[base : base + CHUNK, :]
+        seg_row = segr_ref[:, r * CHUNK : (r + 1) * CHUNK]
+        running = cb_ref[...] + cw_ref[CONV - 1 : CONV, :] * conv[base : base + CHUNK, :]
+        for offset in range(1, CONV):
+            usable = (segc_ref[base - offset : base - offset + CHUNK, :] == seg_col).astype(jnp.float32)
+            running = running + cw_ref[CONV - 1 - offset : CONV - offset, :] * conv[base - offset : base - offset + CHUNK, :] * usable
+        conv_out = running / (1.0 + jnp.exp(-running))
+        x_part = conv_out[:, :HEAD_DIM]
+        b_part = conv_out[:, HEAD_DIM : HEAD_DIM + STATE]
+        c_part = conv_out[:, HEAD_DIM + STATE :]
+
+        raw = jnp.sum(pdt_in[:, r, :], axis=0, keepdims=True) + par_ref[1:2, :]
+        step_row = jnp.maximum(raw, 0.0) + jnp.log1p(jnp.exp(-jnp.abs(raw)))
+        decay_row = -par_ref[0:1, :] * step_row
+        t_at = lax.broadcasted_iota(jnp.int32, (CHUNK, CHUNK), 0)
+        s_at = lax.broadcasted_iota(jnp.int32, (CHUNK, CHUNK), 1)
+        step_col = jnp.sum(jnp.where(t_at == s_at, step_row, 0.0), axis=1, keepdims=True)
+        cum_col = jnp.sum(jnp.where(t_at >= s_at, decay_row, 0.0), axis=1, keepdims=True)
+        cum_row = jnp.sum(jnp.where(t_at == s_at, cum_col, 0.0), axis=0, keepdims=True)
+        allowed = (t_at >= s_at) & (seg_col == seg_row)
+        weights = jnp.where(allowed, jnp.exp(jnp.where(allowed, cum_col - cum_row, 0.0)), 0.0)
+        x_scaled = x_part * step_col
+        scores = dot32(c_part, b_part, ((1,), (1,)))
+        y = dot32(scores * weights, x_scaled, ((1,), (0,)))
+        last_seg = segc_ref[base + CHUNK - 1 : base + CHUNK, :]
+        cum_last = cum_col[CHUNK - 1 : CHUNK, :]
+        if r > 0:
+            prev_seg = segc_ref[base - 1 : base, :]
+            reaches = (seg_col == prev_seg).astype(jnp.float32) * jnp.exp(cum_col)
+            y = y + reaches * dot32(c_part, state[...], ((1,), (1,)))
+        if r < chunks - 1:
+            end_weight = jnp.exp(cum_last - cum_col) * (seg_col == last_seg).astype(jnp.float32)
+            local = dot32(x_scaled * end_weight, b_part, ((0,), (0,)))
+            if r == 0:
+                state[...] = local
+            else:
+                state[...] = (last_seg == prev_seg).astype(jnp.float32) * jnp.exp(cum_last) * state[...] + local
+        gated = y * (gate_part / (1.0 + jnp.exp(-gate_part)))
+        normed = gated * lax.rsqrt(jnp.mean(gated * gated, axis=1, keepdims=True) + 1e-05)
+        gat[r, me] = normed.astype(jnp.bfloat16)
+
+    def g_copy(r, origin, route, dev):
+        return remote(gat.at[r, origin], gat.at[r, origin], gsend.at[r, route], grecv.at[r, origin], dev)
+
+    def g_first(r):
+        g_copy(r, me, 0, xnb).start()
+        g_copy(r, me, 1, sib).start()
+
+        @pl.when(z < 3)
+        def _():
+            g_copy(r, me, 2, up_dev).start()
+
+        @pl.when(z > 0)
+        def _():
+            g_copy(r, me, 3, down_dev).start()
+
+    def g_relay(r):
+        for dist in range(1, 4):
+            for route, sign in ((4, -1), (12, 1)):
+                origin = me + 4 * sign * dist
+                source = z + sign * dist
+
+                @pl.when((source >= 0) & (source <= 3))
+                def _(origin=origin, route=route, sign=sign, dist=dist):
+                    g_copy(r, origin, 0, xnb).wait_recv()
+                    g_copy(r, origin, route + 2 * (dist - 1), xnb).start()
+                    g_copy(r, origin, route + 1 + 2 * (dist - 1), sib).start()
+                    if sign < 0 and dist < 3:
+
+                        @pl.when(z < 3)
+                        def _():
+                            g_copy(r, origin, 20 + dist, up_dev).start()
+
+                    if sign > 0 and dist < 3:
+
+                        @pl.when(z > 0)
+                        def _():
+                            g_copy(r, origin, 23 + dist, down_dev).start()
+
+        for j in range(4):
+            origin = head_of(1 - x, j, core)
+            g_copy(r, origin, 0, sib).wait_recv()
+            g_copy(r, origin, 27 + j, sib).start()
+
+    def g_finish(r):
+        for j in range(8):
+            g_copy(r, j * 2 + 1 - core, 0, sib).wait_recv()
+        total = jnp.zeros((CHUNK, out_ref.shape[1]), jnp.float32)
+        for h in range(0, heads, 2):
+            pair = jnp.concatenate([gat[r, h], gat[r, h + 1]], axis=1)
+            total = total + jnp.dot(pair, owbuf[h * HEAD_DIM : (h + 2) * HEAD_DIM, :], preferred_element_type=jnp.float32)
+        out_ref[r * CHUNK : (r + 1) * CHUNK, :] = total.astype(out_ref.dtype)
+
+    def drain():
+        sib_tok.wait_send()
+        for k, side in pairs:
+            sib_w(k, side).wait_send()
+        for step in range(1, heads):
+            dtw_copy(step, False).wait_send()
+            pdt_copy(step, False).wait_send()
+        for r in range(chunks):
+            for k in range(4):
+                x_copy(r, k).wait_send()
+            for k in range(3):
+                z_copy(r, 0, k, ur, urs, up_dev).wait_send()
+            for route in (0, 1, 27, 28, 29, 30):
+                g_copy(r, me, route, sib).wait_send()
+
+            @pl.when(z < 3)
+            def _():
+                g_copy(r, me, 2, sib).wait_send()
+
+            @pl.when(z > 0)
+            def _():
+                g_copy(r, me, 3, sib).wait_send()
+
+            for dist in range(1, 4):
+                for route, sign in ((4, -1), (12, 1)):
+                    source = z + sign * dist
+
+                    @pl.when((source >= 0) & (source <= 3))
+                    def _(route=route, sign=sign, dist=dist):
+                        g_copy(r, me, route + 2 * (dist - 1), sib).wait_send()
+                        g_copy(r, me, route + 1 + 2 * (dist - 1), sib).wait_send()
+                        if dist < 3:
+
+                            @pl.when((z < 3) if sign < 0 else (z > 0))
+                            def _():
+                                g_copy(r, me, (20 if sign < 0 else 23) + dist, sib).wait_send()
+
+    conv[0:8, :] = jnp.zeros((8, conv.shape[1]), jnp.float32)
+    x_phase(0)
+    step_phase()
+    z_phase(0)
+    for r in range(1, chunks):
+        x_phase(r)
+        if r == 1:
+            for step in range(1, heads):
+                pdt_copy(step, True).wait_recv()
+        z_phase(r)
+        block_phase(r - 1)
+        g_first(r - 1)
+        if r > 1:
+            g_relay(r - 2)
+            if r == 2:
+                local_ow.wait()
+    block_phase(chunks - 1)
+    g_first(chunks - 1)
+    g_relay(chunks - 2)
+    g_finish(0)
+    g_relay(chunks - 1)
+    for r in range(1, chunks):
+        g_finish(r)
+    drain()
+
+
+def fused_body(
+    tokens, segment_ids, in_weight, dt_weight, conv_weight, conv_bias, a_rate, dt_bias, out_weight
+):
+    heads = 16
+    length, depth = tokens.shape
+    chunks = length // CHUNK
+    dtw = jnp.pad(dt_weight.astype(jnp.float32).reshape(heads, depth // 128, 128), ((0, 0), (0, 8 - depth // 128), (0, 0)))
+    segc = jnp.concatenate([jnp.full((8,), -1, jnp.int32), segment_ids]).reshape(length + 8, 1)
+    par = jnp.broadcast_to(jnp.concatenate([a_rate, dt_bias])[:, None], (2, 128))
+    vm = pl.BlockSpec(memory_space=pltpu.VMEM)
+    hbm = pl.BlockSpec(memory_space=pl.ANY)
+    dma = pltpu.SemaphoreType.DMA
+    piece = (chunks, 4, CHUNK, BLOCK_COLS)
+    return pl.pallas_call(
+        fused,
+        out_shape=jax.ShapeDtypeStruct((length, out_weight.shape[1]), jnp.bfloat16),
+        in_specs=[vm, hbm, vm, vm, vm, vm, vm, vm, hbm],
+        out_specs=vm,
+        scratch_shapes=[
+            pltpu.VMEM((2, length, depth), jnp.bfloat16),
+            pltpu.VMEM((8, 2 * depth, BLOCK_COLS), jnp.bfloat16),
+            pltpu.VMEM(out_weight.shape, jnp.bfloat16),
+            pltpu.VMEM((heads, 8, 128), jnp.float32),
+            pltpu.VMEM((heads, 8, 128), jnp.float32),
+            pltpu.VMEM((heads, 8, 128), jnp.float32),
+            pltpu.VMEM(piece, jnp.int16),
+            pltpu.VMEM(piece, jnp.int16),
+            pltpu.VMEM(piece, jnp.int16),
+            pltpu.VMEM(piece, jnp.int16),
+            pltpu.VMEM(piece, jnp.int16),
+            pltpu.VMEM((chunks, CHUNK, BLOCK_COLS), jnp.float32),
+            pltpu.VMEM((CHUNK, BLOCK_COLS), jnp.float32),
+            pltpu.VMEM((length + 8, HEAD_DIM + 2 * STATE), jnp.float32),
+            pltpu.VMEM((CHUNK, BLOCK_COLS), jnp.bfloat16),
+            pltpu.VMEM((chunks, heads, CHUNK, HEAD_DIM), jnp.bfloat16),
+            pltpu.VMEM((HEAD_DIM, STATE), jnp.float32),
+            dma((12,)), dma((8,)), dma((8,)), dma((2,)),
+            dma((heads,)), dma((heads,)), dma((heads,)), dma((heads,)),
+            dma((chunks, 4)), dma((chunks, 4)), dma((chunks, 4)), dma((chunks, 4)), dma((chunks, 4)),
+            dma((chunks, 32)), dma((chunks, heads)),
+        ],
+        compiler_params=pltpu.CompilerParams(
+            collective_id=0, has_side_effects=True, vmem_limit_bytes=48 * 1024 * 1024
+        ),
+    )(
+        tokens, in_weight, dtw, segc, segment_ids.reshape(1, length),
+        conv_weight, conv_bias.reshape(1, -1), par, out_weight,
+    )
+
+
 def solution(mesh):
     return jax.shard_map(
-        body,
+        fused_body if mesh.shape["head"] == 16 else body,
         mesh=mesh,
         in_specs=(
             P("groups", "head"),

time: 225 us -> 92.8 us (0.41)
  waiting for transfers between devices: 104 us -> 0 us
  Pallas kernels: 0 us -> 83.8 us
  blocking collectives: 56.5 us -> 0 us
  matrix products: 20.2 us -> 0 us
  between operations: 14.9 us -> 1.34 us
  other arithmetic: 13.1 us -> 0.93 us
  starting transfers between devices: 7.36 us -> 0 us
    pallas_call x0 -> x1, Pallas kernels: none -> 83.8 us  [fused_body(): pl.pallas_call(fused, out_shape=jax.ShapeDtypeStruct((length, out_weight....]
    reduce_scatter x1 -> x0, waiting for transfers between devices: 61.7 us -> none  [body(): lax.psum_scatter(proj_part, 'head', scatter_dimension=1, tiled=True)]
    unnamed x1 -> x0, blocking collectives: 56.5 us -> none
    all_gather x1 -> x0, waiting for transfers between devices: 39.5 us -> none  [body(): all_normed = lax.all_gather(normed, 'head', axis=1, tiled=True)]
    dot_general x7 -> x0, matrix products: 20.2 us -> none  [the longest x1 11.6 us: body(): proj_part = jnp.dot(tokens, in_weight, preferred_element_type=jnp.float32)]
    all_to_all x1 -> x0, starting transfers between devices: 7.32 us -> none  [body(): lax.all_to_all(dt_weight, 'head', split_axis=0, concat_axis=1, tiled=True)]
    add x3 -> x0, other arithmetic: 4.43 us -> none  [pass_on(): return (through_block[:, None, None] * carried + local_block, carried)]
    dynamic_slice x3 -> x0, local copies, waits for them, and re-layouts: 3.75 us -> none  [block_scan(): _, entering = lax.scan(pass_on, zero_state, (through, local_state))]
  transfers between devices with their start and end apart: 3 -> 0, of which waited for: 3 -> 0; matrix products, arithmetic and copies ran while one was open for 3% -> 0% of each run, Pallas kernels for 0% -> 0%
where the time goes in v1:
time: 92.8 us; the launch traced here: 92.4 us
  Pallas kernels  83.8 us (90%)
  local copies, waits for them, and re-layouts  6.35 us (7%)
  between operations  1.34 us (1%)
  other arithmetic  0.93 us (1%)
    pallas_call x1, Pallas kernels, fused_body(): pl.pallas_call(fused, out_shape=jax.ShapeDtypeStruct((length, out_weight....  83.8 us
    unnamed x7, local copies, waits for them, and re-layouts  4.02 us

profile of v1, /device:TPU:1, one launch (start us, length us, event | category | flops | bytes accessed | tf_op | source)
XLA Modules:
  0.0 92.4 jit_solution(15336508969083074880)
XLA Ops:
  1.3 0.1 pad_maximum_fusion
  1.4 0.1 broadcast_in_dim.2.par_ref
  1.4 0.7 reshape.17.cb_ref
  2.1 0.7 reshape.16.segr_ref
  2.8 0.8 concatenate.6
  3.6 0.8 reduce
  4.4 0.1 copy.10.segc_ref
  4.6 0.0 copy-start
  4.6 1.6 %copy-done = bf16[2048,512]{1,0:T(8,128)(2,1)S(1)} copy-done((bf16[2048,512]{1,0:T(8,128)(2,1)S(1)}, bf16[2048,512]{1,0:T(8,128)(2,1)}, u32[]{:S(2)}) %copy-start) | copy-done | bytes 2097176
  6.2 0.0 copy-start.1
  6.2 1.0 %copy-done.1 = bf16[384,512]{1,0:T(8,128)(2,1)S(1)} copy-done((bf16[384,512]{1,0:T(8,128)(2,1)S(1)}, bf16[384,512]{1,0:T(8,128)(2,1)}, u32[]{:S(2)}) %copy-start.1) | copy-done | bytes 393240
  7.2 0.0 copy-start.2
  7.2 0.7 copy-done.2
  7.9 83.8 %shard_map.91 = bf16[384,512]{1,0:T(8,128)(2,1)S(1)} custom-call(bf16[384,512]{1,0:T(8,128)(2,1)S(1)} %copy-done.1, bf16[512,8192]{1,0:T(8,128)(2,1)} %w_ref.1, f32[16,8,128]{2,1,0:T(8,128)S(1)} %pad_convert_fusion.dtw_ref, s32[392,1]{1,0:T(8,128)S(1)} %copy.10.segc_ref, s32[1,384]{1,0:T(1,128)S(1)} %reshape.16.segr_ref, f32[4,384]{1,0:T(4,128)S(1)} %copy-done.2, ...), custom_call_target="tpu_custom_call" | custom-call | tf_op jit(solution)/shard_map/pallas_call | solution.py:466
  91.7 0.7 copy.14
  (1 shorter events, 0.0 us)
Async XLA Ops:
  4.6 1.6 %copy-start = (bf16[2048,512]{1,0:T(8,128)(2,1)S(1)}, bf16[2048,512]{1,0:T(8,128)(2,1)}, u32[]{:S(2)}) copy-start(bf16[2048,512]{1,0:T(8,128)(2,1)} %ow_ref.1) | copy-start | bytes 6291460
  6.2 1.0 %copy-start.1 = (bf16[384,512]{1,0:T(8,128)(2,1)S(1)}, bf16[384,512]{1,0:T(8,128)(2,1)}, u32[]{:S(2)}) copy-start(bf16[384,512]{1,0:T(8,128)(2,1)} %tok_ref.1) | copy-start | bytes 1179652
  7.2 0.7 copy-start.2

commit v2 on v1

--- a/solution.py
+++ b/solution.py
@@ -111,7 +111,7 @@
     return mixed_out.astype(jnp.bfloat16)
 
 
-CHUNK = 128
+CHUNKS = ((0, 64), (64, 128), (192, 128), (320, 64))
 BLOCK_COLS = 2 * HEAD_DIM + 2 * STATE
 CODE_STEP = 1170.0
 CODE_LOW = 16.0
@@ -132,11 +132,12 @@
 
 
 def fused(
-    tok_ref, w_ref, dtw_ref, segc_ref, segr_ref, cw_ref, cb_ref, par_ref, ow_ref, out_ref,
-    tok, wbuf, owbuf, dtw, pdt_out, pdt_in, xs, xr, zs, ur, dr, acc, part, conv, gate, gat, state,
-    loc_sem, wsend, wrecv, tsem, dws, dwr, pds, pdr, xss, xrs, zss, urs, drs, gsend, grecv,
+    tok_ref, w_ref, dtw_ref, small_ref, ow_ref, out_ref,
+    tok, wbuf, owbuf, dtw, pdt_out, pdt_in, xs, xr, zs, ur, dr, zs2, ur2, dr2, acc, part, conv, gate, gat, state, small, segc,
+    loc_sem, wsend, wrecv, tsem, dws, dwr, pds, pdr, xss, xrs, zss, urs, drs, zss2, urs2, drs2, gsend, grecv,
 ):
-    chunks = tok_ref.shape[0] // CHUNK
+    chunks = len(CHUNKS)
+    length = tok_ref.shape[0]
     heads = dtw_ref.shape[0]
     depth = tok_ref.shape[1]
     me = lax.axis_index("head")
@@ -178,78 +179,122 @@
             wbuf.at[slot, pl.ds(depth, depth)], wsend.at[slot], wrecv.at[slot], sib,
         )
 
-    pairs = [(k, side) for side in range(2) for k in range(4)]
+    pairs = [(k, side) for k in range(4) for side in range(2)]
     local_tok = pltpu.make_async_copy(tok_ref, tok.at[0], loc_sem.at[8])
     local_tok.start()
+    local_small = pltpu.make_async_copy(small_ref, small, loc_sem.at[12])
+    local_small.start()
     for k, side in pairs:
         local_w(k, side).start()
     local_ow = pltpu.make_async_copy(ow_ref, owbuf, loc_sem.at[9])
     local_ow.start()
     pl.semaphore_wait(barrier, heads - 1)
 
+    def dtw_copy(step, incoming):
+        other = lax.rem(me + step, heads)
+        return remote(dtw_ref.at[other], dtw.at[other if incoming else me], dws.at[step], dwr.at[heads - step if incoming else step], other)
+
     sib_tok = remote(tok_ref, tok.at[1], tsem.at[0], tsem.at[1], sib)
     sib_tok.start()
     for k, side in pairs:
         sib_w(k, side).start()
-
-    def dtw_copy(step, incoming):
-        other = lax.rem(me + step, heads)
-        return remote(dtw_ref.at[other], dtw.at[other if incoming else me], dws.at[step], dwr.at[heads - step if incoming else step], other)
-
-    for step in range(1, heads):
-        dtw_copy(step, False).start()
+        if k == 0:
+            for step in range(1 + side, heads, 2):
+                dtw_copy(step, False).start()
+
     own_dtw = pltpu.make_async_copy(dtw_ref.at[me], dtw.at[me], loc_sem.at[10])
     own_dtw.start()
     local_tok.wait()
     sib_tok.wait_recv()
 
-    def product(slot, r):
-        rows = pl.ds(r * CHUNK, CHUNK)
+    ready = set()
+
+    def product(k, side, r):
+        start, size = CHUNKS[r]
+        slot = side * 4 + k
+        if slot not in ready:
+            ready.add(slot)
+            local_w(k, side).wait()
+            sib_w(k, side).wait_recv()
+        rows = pl.ds(start, size)
         return jnp.dot(tok[0, rows, :], wbuf[slot, :depth], preferred_element_type=jnp.float32) + jnp.dot(
             tok[1, rows, :], wbuf[slot, depth:], preferred_element_type=jnp.float32
         )
 
     def x_copy(r, k):
-        return remote(xs.at[r, k], xr.at[r, k], xss.at[r, k], xrs.at[r, k], xnb)
-
-    def z_copy(r, d, k, buf, sems, dev):
-        return remote(zs.at[r, k], buf.at[r, d], zss.at[r, k], sems.at[r, d], dev)
+        rows = pl.ds(0, CHUNKS[r][1])
+        return remote(xs.at[r, k, rows], xr.at[r, k, rows], xss.at[r, k], xrs.at[r, k], xnb)
+
+    side_bufs = ((zs2, zss2, ur2, urs2, dr2, drs2), (zs, zss, ur, urs, dr, drs))
+
+    def z_copy(r, d, k, up, side=1):
+        rows = pl.ds(0, CHUNKS[r][1])
+        out, out_sems, ub, us, db, ds = side_bufs[side]
+        buf, sems, dev = (ub, us, up_dev) if up else (db, ds, down_dev)
+        return remote(out.at[r, k, rows], buf.at[r, d, rows], out_sems.at[r, k], sems.at[r, d], dev)
+
+    def z_sent(r, k, side=1):
+        z_copy(r, 0, k, True, side).wait_send()
+
+    def z_received(r, d, side, up):
+        size = CHUNKS[r][1]
+        z_copy(r, d, 0, up, side).wait_recv()
+        return decode(side_bufs[side][2 if up else 4][r, d, :size])
+
+    def x_step(r, k):
+        xs[r, k, : CHUNKS[r][1]] = encode(product(k, 0, r))
+        x_copy(r, k).start()
 
     def x_phase(r):
         for k in range(4):
-            if r == 0:
-                local_w(k, 0).wait()
-                sib_w(k, 0).wait_recv()
-            xs[r, k] = encode(product(k, r))
-            x_copy(r, k).start()
+            x_step(r, k)
+
+    def pass_on(r, k, side, mine):
+        size = CHUNKS[r][1]
+        d = order(k)
+        part[:size] = mine
+        for up in (True, False):
+
+            @pl.when((d > z) if up else (d < z))
+            def _(up=up):
+                @pl.when((z != 0) if up else (z != 3))
+                def _():
+                    part[:size] += z_received(r, d, side, up)
+
+                side_bufs[side][0][r, k, :size] = encode(part[:size])
+                z_copy(r, d, k, up, side).start()
+
+    def arrive(r, side, total, size):
+        for up in (True, False):
+
+            @pl.when((z != 0) if up else (z != 3))
+            def _(up=up):
+                total[:size] += z_received(r, z, side, up)
 
     def z_phase(r):
+        size = CHUNKS[r][1]
         for k in range(4):
-            if r == 0:
-                local_w(k, 1).wait()
-                sib_w(k, 1).wait_recv()
-            d = order(k)
-            mine = product(4 + k, r)
+            mine = product(k, 1, r)
             x_copy(r, k).wait_recv()
-            mine = mine + decode(xr[r, k])
+            mine = mine + decode(xr[r, k, :size])
             if k == 3:
-                acc[r] = mine
+                acc[r, :size] = mine
             else:
-                part[...] = mine
-                for buf, sems, dev, here, first in (
-                    (ur, urs, up_dev, d > z, z == 0),
-                    (dr, drs, down_dev, d < z, z == 3),
-                ):
-
-                    @pl.when(here)
-                    def _(buf=buf, sems=sems, dev=dev, first=first):
-                        @pl.when(jnp.logical_not(first))
-                        def _():
-                            z_copy(r, d, k, buf, sems, dev).wait_recv()
-                            part[...] += decode(buf[r, d])
-
-                        zs[r, k] = encode(part[...])
-                        z_copy(r, d, k, buf, sems, dev).start()
+                pass_on(r, k, 1, mine)
+
+    def z_first_step(k):
+        for side in range(2):
+            if k < 3:
+                pass_on(0, k, side, product(k, side, 0))
+            elif side == 1:
+                acc[0, : CHUNKS[0][1]] = product(k, 1, 0)
+
+    def z_first_end():
+        size = CHUNKS[0][1]
+        part[:size] = product(3, 0, 0)
+        arrive(0, 0, part, size)
+        xs[0, 0, :size] = encode(part[:size])
+        x_copy(0, 0).start()
 
     def pdt_copy(step, incoming):
         other = lax.rem(me + step, heads)
@@ -265,10 +310,9 @@
                 dtw[:, j, :].astype(jnp.bfloat16), tok[0, :, j * 128 : (j + 1) * 128],
                 (((1,), (1,)), ((), ())), preferred_element_type=jnp.float32,
             )
-        for r in range(chunks):
-            pdt_out[:, r, :] = total[:, r * CHUNK : (r + 1) * CHUNK]
-        for r in range(chunks, 8):
-            pdt_out[:, r, :] = jnp.zeros((heads, 128), jnp.float32)
+        pdt_out[...] = jnp.zeros(pdt_out.shape, jnp.float32)
+        for r, (start, size) in enumerate(CHUNKS):
+            pdt_out[:, r, :size] = total[:, start : start + size]
         for step in range(1, heads):
             pdt_copy(step, False).start()
         own = pltpu.make_async_copy(pdt_out.at[me], pdt_in.at[me], loc_sem.at[11])
@@ -281,33 +325,31 @@
         return lax.dot_general(a, b, (dims, ((), ())), precision=top, preferred_element_type=jnp.float32)
 
     def block_phase(r):
-        for edge, buf, sems, dev in ((0, ur, urs, up_dev), (3, dr, drs, down_dev)):
-
-            @pl.when(z != edge)
-            def _(buf=buf, sems=sems, dev=dev):
-                z_copy(r, z, 3, buf, sems, dev).wait_recv()
-                acc[r] += decode(buf[r, z])
-
-        gate[...] = acc[r].astype(jnp.bfloat16)
-        projected = gate[...].astype(jnp.float32)
-        base = 8 + r * CHUNK
+        start, CHUNK = CHUNKS[r]
+        arrive(r, 1, acc.at[r], CHUNK)
+        if r == 0:
+            x_copy(0, 0).wait_recv()
+            acc[0, :CHUNK] += decode(xr[0, 0, :CHUNK])
+        gate[:CHUNK] = acc[r, :CHUNK].astype(jnp.bfloat16)
+        projected = gate[:CHUNK].astype(jnp.float32)
+        base = 8 + start
         conv[base : base + CHUNK, :HEAD_DIM] = projected[:, :HEAD_DIM]
         conv[base : base + CHUNK, HEAD_DIM:] = projected[:, 2 * HEAD_DIM :]
         gate_part = projected[:, HEAD_DIM : 2 * HEAD_DIM]
-        seg_col = segc_ref[base : base + CHUNK, :]
-        seg_row = segr_ref[:, r * CHUNK : (r + 1) * CHUNK]
-        running = cb_ref[...] + cw_ref[CONV - 1 : CONV, :] * conv[base : base + CHUNK, :]
+        seg_col = segc[base : base + CHUNK, :]
+        seg_row = small[5:6, start : start + CHUNK]
+        running = small[4:5, :] + small[CONV - 1 : CONV, :] * conv[base : base + CHUNK, :]
         for offset in range(1, CONV):
-            usable = (segc_ref[base - offset : base - offset + CHUNK, :] == seg_col).astype(jnp.float32)
-            running = running + cw_ref[CONV - 1 - offset : CONV - offset, :] * conv[base - offset : base - offset + CHUNK, :] * usable
+            usable = (segc[base - offset : base - offset + CHUNK, :] == seg_col).astype(jnp.float32)
+            running = running + small[CONV - 1 - offset : CONV - offset, :] * conv[base - offset : base - offset + CHUNK, :] * usable
         conv_out = running / (1.0 + jnp.exp(-running))
         x_part = conv_out[:, :HEAD_DIM]
         b_part = conv_out[:, HEAD_DIM : HEAD_DIM + STATE]
         c_part = conv_out[:, HEAD_DIM + STATE :]
 
-        raw = jnp.sum(pdt_in[:, r, :], axis=0, keepdims=True) + par_ref[1:2, :]
+        raw = jnp.sum(pdt_in[:, r, :CHUNK], axis=0, keepdims=True) + small[7:8, :CHUNK]
         step_row = jnp.maximum(raw, 0.0) + jnp.log1p(jnp.exp(-jnp.abs(raw)))
-        decay_row = -par_ref[0:1, :] * step_row
+        decay_row = -small[6:7, :CHUNK] * step_row
         t_at = lax.broadcasted_iota(jnp.int32, (CHUNK, CHUNK), 0)
         s_at = lax.broadcasted_iota(jnp.int32, (CHUNK, CHUNK), 1)
         step_col = jnp.sum(jnp.where(t_at == s_at, step_row, 0.0), axis=1, keepdims=True)
@@ -318,10 +360,10 @@
         x_scaled = x_part * step_col
         scores = dot32(c_part, b_part, ((1,), (1,)))
         y = dot32(scores * weights, x_scaled, ((1,), (0,)))
-        last_seg = segc_ref[base + CHUNK - 1 : base + CHUNK, :]
+        last_seg = segc[base + CHUNK - 1 : base + CHUNK, :]
         cum_last = cum_col[CHUNK - 1 : CHUNK, :]
         if r > 0:
-            prev_seg = segc_ref[base - 1 : base, :]
+            prev_seg = segc[base - 1 : base, :]
             reaches = (seg_col == prev_seg).astype(jnp.float32) * jnp.exp(cum_col)
             y = y + reaches * dot32(c_part, state[...], ((1,), (1,)))
         if r < chunks - 1:
@@ -333,59 +375,42 @@
                 state[...] = (last_seg == prev_seg).astype(jnp.float32) * jnp.exp(cum_last) * state[...] + local
         gated = y * (gate_part / (1.0 + jnp.exp(-gate_part)))
         normed = gated * lax.rsqrt(jnp.mean(gated * gated, axis=1, keepdims=True) + 1e-05)
-        gat[r, me] = normed.astype(jnp.bfloat16)
+        gat[me, start : start + CHUNK] = normed.astype(jnp.bfloat16)
 
     def g_copy(r, origin, route, dev):
-        return remote(gat.at[r, origin], gat.at[r, origin], gsend.at[r, route], grecv.at[r, origin], dev)
+        start, size = CHUNKS[r]
+        here = gat.at[origin, pl.ds(start, size)]
+        return remote(here, here, gsend.at[r, route], grecv.at[r, origin], dev)
+
+    def column(j):
+        return lax.rem(z + j, 4) * 4 + lax.rem(me, 4)
 
     def g_first(r):
+        for j in range(1, 4):
+            g_copy(r, me, j, column(j)).start()
         g_copy(r, me, 0, xnb).start()
-        g_copy(r, me, 1, sib).start()
-
-        @pl.when(z < 3)
-        def _():
-            g_copy(r, me, 2, up_dev).start()
-
-        @pl.when(z > 0)
-        def _():
-            g_copy(r, me, 3, down_dev).start()
+        g_copy(r, me, 4, sib).start()
 
     def g_relay(r):
-        for dist in range(1, 4):
-            for route, sign in ((4, -1), (12, 1)):
-                origin = me + 4 * sign * dist
-                source = z + sign * dist
-
-                @pl.when((source >= 0) & (source <= 3))
-                def _(origin=origin, route=route, sign=sign, dist=dist):
-                    g_copy(r, origin, 0, xnb).wait_recv()
-                    g_copy(r, origin, route + 2 * (dist - 1), xnb).start()
-                    g_copy(r, origin, route + 1 + 2 * (dist - 1), sib).start()
-                    if sign < 0 and dist < 3:
-
-                        @pl.when(z < 3)
-                        def _():
-                            g_copy(r, origin, 20 + dist, up_dev).start()
-
-                    if sign > 0 and dist < 3:
-
-                        @pl.when(z > 0)
-                        def _():
-                            g_copy(r, origin, 23 + dist, down_dev).start()
-
-        for j in range(4):
-            origin = head_of(1 - x, j, core)
+        for j in (1, 3, 2):
+            origin = column(j)
+            g_copy(r, origin, 0, xnb).wait_recv()
+            g_copy(r, origin, 4 + j, xnb).start()
+            g_copy(r, origin, 7 + j, sib).start()
+        for j in (0, 1, 3, 2):
+            origin = column(j) + 2 - 4 * x
             g_copy(r, origin, 0, sib).wait_recv()
-            g_copy(r, origin, 27 + j, sib).start()
+            g_copy(r, origin, 11 + j, sib).start()
 
     def g_finish(r):
         for j in range(8):
             g_copy(r, j * 2 + 1 - core, 0, sib).wait_recv()
-        total = jnp.zeros((CHUNK, out_ref.shape[1]), jnp.float32)
+        start, size = CHUNKS[r]
+        total = jnp.zeros((size, out_ref.shape[1]), jnp.float32)
         for h in range(0, heads, 2):
-            pair = jnp.concatenate([gat[r, h], gat[r, h + 1]], axis=1)
+            pair = jnp.concatenate([gat[h, start : start + size], gat[h + 1, start : start + size]], axis=1)
             total = total + jnp.dot(pair, owbuf[h * HEAD_DIM : (h + 2) * HEAD_DIM, :], preferred_element_type=jnp.float32)
-        out_ref[r * CHUNK : (r + 1) * CHUNK, :] = total.astype(out_ref.dtype)
+        out_ref[start : start + size, :] = total.astype(out_ref.dtype)
 
     def drain():
         sib_tok.wait_send()
@@ -395,58 +420,59 @@
             dtw_copy(step, False).wait_send()
             pdt_copy(step, False).wait_send()
         for r in range(chunks):
-            for k in range(4):
+            for k in range(4 if r else 1):
                 x_copy(r, k).wait_send()
-            for k in range(3):
-                z_copy(r, 0, k, ur, urs, up_dev).wait_send()
-            for route in (0, 1, 27, 28, 29, 30):
+            for side in range(2 if r == 0 else 1):
+                for k in range(3):
+                    z_sent(r, k, 0 if side else 1)
+            for route in range(15):
                 g_copy(r, me, route, sib).wait_send()
 
-            @pl.when(z < 3)
-            def _():
-                g_copy(r, me, 2, sib).wait_send()
-
-            @pl.when(z > 0)
-            def _():
-                g_copy(r, me, 3, sib).wait_send()
-
-            for dist in range(1, 4):
-                for route, sign in ((4, -1), (12, 1)):
-                    source = z + sign * dist
-
-                    @pl.when((source >= 0) & (source <= 3))
-                    def _(route=route, sign=sign, dist=dist):
-                        g_copy(r, me, route + 2 * (dist - 1), sib).wait_send()
-                        g_copy(r, me, route + 1 + 2 * (dist - 1), sib).wait_send()
-                        if dist < 3:
-
-                            @pl.when((z < 3) if sign < 0 else (z > 0))
-                            def _():
-                                g_copy(r, me, (20 if sign < 0 else 23) + dist, sib).wait_send()
-
     conv[0:8, :] = jnp.zeros((8, conv.shape[1]), jnp.float32)
-    x_phase(0)
+    local_small.wait()
+    segc[0:8, :] = jnp.full((8, 1), -1.0, jnp.float32)
+    for start, size in CHUNKS:
+        square = lax.broadcasted_iota(jnp.int32, (size, size), 0) == lax.broadcasted_iota(jnp.int32, (size, size), 1)
+        segc[8 + start : 8 + start + size, :] = jnp.sum(
+            jnp.where(square, small[5:6, start : start + size], 0.0), axis=1, keepdims=True
+        )
+    x_step(1, 0)
+    z_first_step(0)
+    x_step(1, 1)
     step_phase()
-    z_phase(0)
-    for r in range(1, chunks):
-        x_phase(r)
-        if r == 1:
-            for step in range(1, heads):
-                pdt_copy(step, True).wait_recv()
-        z_phase(r)
-        block_phase(r - 1)
-        g_first(r - 1)
-        if r > 1:
-            g_relay(r - 2)
-            if r == 2:
-                local_ow.wait()
-    block_phase(chunks - 1)
-    g_first(chunks - 1)
-    g_relay(chunks - 2)
+    x_step(1, 2)
+    z_first_step(1)
+    x_step(1, 3)
+    x_step(2, 0)
+    z_first_step(2)
+    x_step(2, 1)
+    z_first_step(3)
+    z_first_end()
+    x_step(2, 2)
+    x_step(2, 3)
+    z_phase(1)
+    for step in range(1, heads):
+        pdt_copy(step, True).wait_recv()
+    block_phase(0)
+    g_first(0)
+    x_phase(3)
+    z_phase(2)
+    block_phase(1)
+    g_first(1)
+    g_relay(0)
+    local_ow.wait()
+    block_phase(2)
+    g_first(2)
+    g_relay(1)
     g_finish(0)
-    g_relay(chunks - 1)
-    for r in range(1, chunks):
-        g_finish(r)
+    z_phase(3)
+    block_phase(3)
+    g_first(3)
+    g_relay(2)
+    g_finish(1)
+    g_relay(3)
+    g_finish(2)
+    g_finish(3)
     drain()
 
 
@@ -455,18 +481,24 @@
 ):
     heads = 16
     length, depth = tokens.shape
-    chunks = length // CHUNK
+    chunks = len(CHUNKS)
     dtw = jnp.pad(dt_weight.astype(jnp.float32).reshape(heads, depth // 128, 128), ((0, 0), (0, 8 - depth // 128), (0, 0)))
-    segc = jnp.concatenate([jnp.full((8,), -1, jnp.int32), segment_ids]).reshape(length + 8, 1)
-    par = jnp.broadcast_to(jnp.concatenate([a_rate, dt_bias])[:, None], (2, 128))
+    lanes = conv_weight.shape[1]
+    at = lax.broadcasted_iota(jnp.int32, (8, lanes), 0)
+    small = jnp.pad(conv_weight, ((0, 8 - CONV), (0, 0)))
+    seg_lanes = jnp.pad(segment_ids, (0, lanes - length)).astype(jnp.float32)
+    for row, values in ((4, conv_bias), (5, seg_lanes), (6, a_rate), (7, dt_bias)):
+        small = jnp.where(at == row, values[None, :], small)
     vm = pl.BlockSpec(memory_space=pltpu.VMEM)
     hbm = pl.BlockSpec(memory_space=pl.ANY)
     dma = pltpu.SemaphoreType.DMA
-    piece = (chunks, 4, CHUNK, BLOCK_COLS)
+    most = max(size for _, size in CHUNKS)
+    piece = (chunks, 4, most, BLOCK_COLS)
+    first = (1, 4, CHUNKS[0][1], BLOCK_COLS)
     return pl.pallas_call(
         fused,
         out_shape=jax.ShapeDtypeStruct((length, out_weight.shape[1]), jnp.bfloat16),
-        in_specs=[vm, hbm, vm, vm, vm, vm, vm, vm, hbm],
+        in_specs=[hbm, hbm, hbm, hbm, hbm],
         out_specs=vm,
         scratch_shapes=[
             pltpu.VMEM((2, length, depth), jnp.bfloat16),
@@ -480,23 +512,28 @@
             pltpu.VMEM(piece, jnp.int16),
             pltpu.VMEM(piece, jnp.int16),
             pltpu.VMEM(piece, jnp.int16),
-            pltpu.VMEM((chunks, CHUNK, BLOCK_COLS), jnp.float32),
-            pltpu.VMEM((CHUNK, BLOCK_COLS), jnp.float32),
+            pltpu.VMEM(first, jnp.int16),
+            pltpu.VMEM(first, jnp.int16),
+            pltpu.VMEM(first, jnp.int16),
+            pltpu.VMEM((chunks, most, BLOCK_COLS), jnp.float32),
+            pltpu.VMEM((most, BLOCK_COLS), jnp.float32),
             pltpu.VMEM((length + 8, HEAD_DIM + 2 * STATE), jnp.float32),
-            pltpu.VMEM((CHUNK, BLOCK_COLS), jnp.bfloat16),
-            pltpu.VMEM((chunks, heads, CHUNK, HEAD_DIM), jnp.bfloat16),
+            pltpu.VMEM((most, BLOCK_COLS), jnp.bfloat16),
+            pltpu.VMEM((heads, length, HEAD_DIM), jnp.bfloat16),
             pltpu.VMEM((HEAD_DIM, STATE), jnp.float32),
-            dma((12,)), dma((8,)), dma((8,)), dma((2,)),
+            pltpu.VMEM((8, lanes), jnp.float32),
+            pltpu.VMEM((length + 8, 1), jnp.float32),
+            dma((13,)), dma((8,)), dma((8,)), dma((2,)),
             dma((heads,)), dma((heads,)), dma((heads,)), dma((heads,)),
             dma((chunks, 4)), dma((chunks, 4)), dma((chunks, 4)), dma((chunks, 4)), dma((chunks, 4)),
-            dma((chunks, 32)), dma((chunks, heads)),
+            dma((1, 4)), dma((1, 4)), dma((1, 4)),
+            dma((chunks, 16)), dma((chunks, heads)),
         ],
         compiler_params=pltpu.CompilerParams(
-            collective_id=0, has_side_effects=True, vmem_limit_bytes=48 * 1024 * 1024
+            collective_id=0, has_side_effects=True, vmem_limit_bytes=60 * 1024 * 1024
         ),
     )(
-        tokens, in_weight, dtw, segc, segment_ids.reshape(1, length),
-        conv_weight, conv_bias.reshape(1, -1), par, out_weight,
+        tokens, in_weight, dtw, small, out_weight,
     )
 
 

time: 92.8 us -> 85.3 us (0.919)
  Pallas kernels: 83.8 us -> 78.3 us
  local copies, waits for them, and re-layouts: 6.35 us -> 1.77 us
  other arithmetic: 0.93 us -> 3.55 us
    pallas_call x1, Pallas kernels: 83.8 us -> 78.3 us  [fused_body(): pl.pallas_call(fused, out_shape=jax.ShapeDtypeStruct((length, out_weight....]
    unnamed x7 -> x1, local copies, waits for them, and re-layouts: 4.02 us -> 1.77 us
    reshape x3 -> x0, local copies, waits for them, and re-layouts: 1.5 us -> none  [the longest x1 0.68 us: fused_body(): conv_bias.reshape(1, -1)]
    select_n x0 -> x1, other arithmetic: none -> 1.37 us  [fused_body(): small = jnp.where(at == row, values[None, :], small)]
where the time goes in v2:
time: 85.3 us; the launch traced here: 85 us
  Pallas kernels  78.3 us (92%)
  other arithmetic  3.55 us (4%)
  local copies, waits for them, and re-layouts  1.77 us (2%)
  between operations  1.32 us (2%)
    pallas_call x1, Pallas kernels, fused_body(): pl.pallas_call(fused, out_shape=jax.ShapeDtypeStruct((length, out_weight....  78.3 us
    unnamed x1, local copies, waits for them, and re-layouts  1.77 us

profile of v2, /device:TPU:1, one launch (start us, length us, event | category | flops | bytes accessed | tf_op | source)
XLA Modules:
  0.0 85.0 jit_solution(18393705250053396923)
XLA Ops:
  1.3 0.7 convert_element_type.8
  2.0 1.4 %select_select_fusion.small_ref = f32[8,384]{1,0:T(8,128)} fusion(f32[4,384]{1,0:T(4,128)} %param.13, f32[384]{0:T(512)} %param.14, f32[384]{0:T(512)S(1)} %convert_element_type.8, f32[]{:T(128)} %bitcast.3, f32[]{:T(128)} %bitcast.4, pred[8]{0:T(512)(128)(4,1)S(1)} %get-tuple-element.5, pred[8]{0:T(512)(128)(4,1)S(1)} %get-tuple-element.6, ...), kind=kLoop, calls=%fused_computation.1 | loop fusion | flops 12288 | bytes 21544 | tf_op jit(solution)/shard_map/jit(_where)/select_n | solution.py:491
  3.4 0.8 reduce
  4.2 0.6 pad_convert_fusion.dtw_ref
  4.9 78.3 %shard_map.91 = bf16[384,512]{1,0:T(8,128)(2,1)} custom-call(bf16[384,512]{1,0:T(8,128)(2,1)} %tok_ref.1, bf16[512,8192]{1,0:T(8,128)(2,1)} %w_ref.1, f32[16,8,128]{2,1,0:T(8,128)} %pad_convert_fusion.dtw_ref, f32[8,384]{1,0:T(8,128)} %select_select_fusion.small_ref, bf16[2048,512]{1,0:T(8,128)(2,1)} %ow_ref.1), custom_call_target="tpu_custom_call" | custom-call | tf_op jit(solution)/shard_map/pallas_call | solution.py:498
  83.2 1.8 %copy.13 = bf16[384,512]{1,0:T(8,128)(2,1)} copy(bf16[384,512]{1,0:T(8,128)(2,1)} %shard_map.91) | data formatting | bytes 786432
  (2 shorter events, 0.0 us)

commit v3 on v2

--- a/solution.py
+++ b/solution.py
@@ -450,27 +450,27 @@
     z_first_end()
     x_step(2, 2)
     x_step(2, 3)
+    x_phase(3)
     z_phase(1)
+    z_phase(2)
     for step in range(1, heads):
         pdt_copy(step, True).wait_recv()
     block_phase(0)
     g_first(0)
-    x_phase(3)
-    z_phase(2)
     block_phase(1)
     g_first(1)
+    z_phase(3)
     g_relay(0)
-    local_ow.wait()
     block_phase(2)
     g_first(2)
-    g_relay(1)
-    g_finish(0)
-    z_phase(3)
     block_phase(3)
     g_first(3)
+    g_relay(1)
     g_relay(2)
+    local_ow.wait()
+    g_finish(0)
+    g_relay(3)
     g_finish(1)
-    g_relay(3)
     g_finish(2)
     g_finish(3)
     drain()

time: 85.3 us -> 79.9 us (0.937)
  Pallas kernels: 78.3 us -> 72.2 us
    pallas_call x1, Pallas kernels: 78.3 us -> 72.2 us  [fused_body(): pl.pallas_call(fused, out_shape=jax.ShapeDtypeStruct((length, out_weight....]
where the time goes in v3:
time: 79.9 us; the launch traced here: 78.8 us
  Pallas kernels  72.2 us (90%)
  other arithmetic  3.55 us (4%)
  local copies, waits for them, and re-layouts  1.77 us (2%)
  between operations  1.32 us (2%)
    pallas_call x1, Pallas kernels, fused_body(): pl.pallas_call(fused, out_shape=jax.ShapeDtypeStruct((length, out_weight....  72.2 us
    unnamed x1, local copies, waits for them, and re-layouts  1.77 us

profile of v3, /device:TPU:1, one launch (start us, length us, event | category | flops | bytes accessed | tf_op | source)
XLA Modules:
  0.0 78.8 jit_solution(15715725304620545291)
XLA Ops:
  1.3 0.7 convert_element_type.8
  2.0 1.4 %select_select_fusion.small_ref = f32[8,384]{1,0:T(8,128)} fusion(f32[4,384]{1,0:T(4,128)} %param.13, f32[384]{0:T(512)} %param.14, f32[384]{0:T(512)S(1)} %convert_element_type.8, f32[]{:T(128)} %bitcast.3, f32[]{:T(128)} %bitcast.4, pred[8]{0:T(512)(128)(4,1)S(1)} %get-tuple-element.5, pred[8]{0:T(512)(128)(4,1)S(1)} %get-tuple-element.6, ...), kind=kLoop, calls=%fused_computation.1 | loop fusion | flops 12288 | bytes 21544 | tf_op jit(solution)/shard_map/jit(_where)/select_n | solution.py:491
  3.4 0.8 %reduce = bf16[8192]{0:T(1024)(128)(2,1)S(1)} reduce(bf16[8192,1]{0,1:T(2,128)(2,1)} %param.12, bf16[]{:T(256)} %constant.20), dimensions={1}, to_apply=%param.12.reduce_sub_computation | reduce | bytes 32770 | tf_op args[3]
  4.2 0.6 pad_convert_fusion.dtw_ref
  4.9 72.2 %shard_map.91 = bf16[384,512]{1,0:T(8,128)(2,1)} custom-call(bf16[384,512]{1,0:T(8,128)(2,1)} %tok_ref.1, bf16[512,8192]{1,0:T(8,128)(2,1)} %w_ref.1, f32[16,8,128]{2,1,0:T(8,128)} %pad_convert_fusion.dtw_ref, f32[8,384]{1,0:T(8,128)} %select_select_fusion.small_ref, bf16[2048,512]{1,0:T(8,128)(2,1)} %ow_ref.1), custom_call_target="tpu_custom_call" | custom-call | tf_op jit(solution)/shard_map/pallas_call | solution.py:498
  77.0 1.8 %copy.13 = bf16[384,512]{1,0:T(8,128)(2,1)} copy(bf16[384,512]{1,0:T(8,128)(2,1)} %shard_map.91) | data formatting | bytes 786432
  (2 shorter events, 0.0 us)
